TPU v7x, 512 devices: a whole 4x4x16 slice. The times are simulated.
512 devices in a mesh: phase: 4 (over x), expert: 32 (over z_hi, y, core), tensor: 4 (over z_lo).
Axes of the slice: x: 4, y: 4, z: 16 (z_hi: 4, z_lo: 4; z = z_hi * 4 + z_lo), core: 2. Of those that a mesh axis runs over, the one named last changes fastest.
Arguments:
- forward_routes: int32 [4, 2048, 6], P('phase', 'expert'), may hold values from 0 to 95, all different within a row; in each aligned block of 64 rows (0 to 63, 64 to 127, ..., all dimensions but the last counted through in order) at most 6 rows name the same one
- forward_gates: float32 [4, 2048, 6], P('phase', 'expert'), may hold values from 0.05 to 1
- hidden_rows: bfloat16 [4, 96, 32, 6, 1024], P('phase', 'expert', None, None, 'tensor'), may hold values from -6 to 6
- down_weight: bfloat16 [4, 96, 1024, 2560], P('phase', 'expert', 'tensor'), may hold values from -0.1875 to 0.1875
- shared_hidden: bfloat16 [4, 2048, 1536], P('phase', 'expert', 'tensor'), may hold values from -6 to 6
- shared_weight: bfloat16 [4, 1536, 2560], P('phase', 'tensor', 'expert'), may hold values from -0.15625 to 0.15625
- backward_routes: int32 [4, 2048, 6], P('phase', 'expert'), may hold values from 0 to 95, all different within a row; in each aligned block of 64 rows (0 to 63, 64 to 127, ..., all dimensions but the last counted through in order) at most 6 rows name the same one
- backward_gates: float32 [4, 2048, 6], P('phase', 'expert'), may hold values from 0.05 to 1
- cotangent: bfloat16 [4, 2048, 2560], P('phase', 'expert', 'tensor'), may hold values from -6 to 6
Outputs:
- forward_next: bfloat16 [4, 2048, 2560], P('phase', 'expert', 'tensor')
- hidden_grad: bfloat16 [4, 96, 32, 6, 1024], P('phase', 'expert', None, None, 'tensor')
- shared_grad: bfloat16 [4, 2048, 1536], P('phase', 'expert', 'tensor')
Inputs may be any that keep to these rules, and one draw needn't show every extreme that they name: `forward_routes`: each token names 6 different experts. The tokens of one token group (the 64 rows of one device) name any one expert 6 times at most, and some group reaches that. `backward_routes`: as for forward_routes.
All inputs are finite; a program needn't handle non-finite values.
Results may differ from a plain program's by a relative error of at most 0.0049.
Values may be sent and summed in bfloat16 or wider, within the bound.
No kernel may reach another device: no remote copies, remote signals or barrier semaphores. Data moves between devices by JAX's collectives and lax.ppermute only.
A program may use at most 64 MiB of HBM per device.

v0:
```python
import jax
import jax.numpy as jnp
from jax import lax
from jax.sharding import PartitionSpec as P


def in_blocks(array, dim, length):
    before, after = (array.shape[:dim], array.shape[dim + 1 :])
    return jnp.moveaxis(array.reshape(*before, length, -1, *after), dim, 0)


def summed_on_arrival(array, axis, dim):
    parts = in_blocks(array, dim, lax.axis_size(axis))
    arrived = lax.all_to_all(parts, axis, split_axis=0, concat_axis=0, tiled=True)
    return arrived.sum(axis=0)


def shifted(value, axis, steps):
    count = lax.axis_size(axis)
    pairs = [(source, (source + steps) % count) for source in range(count)]
    return lax.ppermute(value, axis, pairs)


def sent_to_all(array, axis):
    length = lax.axis_size(axis)
    return lax.all_to_all(
        jnp.broadcast_to(array[None], (length, *array.shape)), axis, 0, 0, tiled=True
    )


def joined_along(parts, dim):
    parts = jnp.moveaxis(parts, 0, dim)
    dims = parts.shape
    return parts.reshape(*dims[:dim], dims[dim] * dims[dim + 1], *dims[dim + 2 :])


def gathered_copies(array, axis, dim):
    parts = sent_to_all(array, axis)
    return joined_along(parts, dim)


def slot_numbers(routes, experts):
    numbers = jnp.arange(experts, dtype=jnp.int32)
    onehot = (routes[:, :, None] == numbers[None, None, :]).astype(jnp.int32)
    per_token = jnp.sum(onehot, axis=1)
    before = jnp.cumsum(per_token, axis=0) - per_token
    return jnp.sum(onehot * before[:, None, :], axis=2)


def row_positions(routes, experts_here, groups, capacity):
    slot_index = slot_numbers(routes, experts_here * groups)
    holder = routes // experts_here
    within = routes - holder * experts_here
    return ((within * groups + holder) * capacity + slot_index).reshape(-1)


def place_rows(gates, values, positions, total_rows):
    scaled = (gates[:, :, None] * values[:, None, :].astype(jnp.float32)).astype(jnp.bfloat16)
    outgoing = jnp.zeros((total_rows, values.shape[1]), jnp.bfloat16)
    return outgoing.at[positions].set(scaled.reshape(-1, values.shape[1]))


def on_device(
    forward_routes,
    forward_gates,
    hidden_rows,
    down_weight,
    shared_hidden,
    shared_weight,
    backward_routes,
    backward_gates,
    cotangent,
):
    experts_here = down_weight.shape[1]
    features = down_weight.shape[3]
    capacity = hidden_rows.shape[3]
    groups = lax.axis_size("expert")
    token_count = forward_routes.shape[1]
    top_count = forward_routes.shape[2]
    hidden = hidden_rows[0]
    weight = down_weight[0]
    local_shared = shared_hidden[0]
    shared_piece = shared_weight[0]
    shared_part = jnp.dot(
        local_shared,
        lax.all_gather(shared_piece, "expert", axis=1, tiled=True),
        preferred_element_type=jnp.float32,
    )
    fore_positions = row_positions(forward_routes[0], experts_here, groups, capacity)
    fore_gates = forward_gates[0]
    partial_value = jnp.einsum(
        "egmh,ehd->egmd", hidden, weight, preferred_element_type=jnp.float32
    ).astype(jnp.bfloat16)
    arrived = lax.all_to_all(partial_value, "expert", split_axis=1, concat_axis=1, tiled=True)
    picked = arrived.reshape(-1, features)[fore_positions].reshape(token_count, top_count, features)
    summand = shared_part + jnp.sum(picked.astype(jnp.float32) * fore_gates[:, :, None], axis=1)
    summed = summed_on_arrival(summand, "tensor", 1)
    layer_out = summed.astype(jnp.bfloat16)
    handed = shifted(layer_out, "phase", 1)
    cotangent_whole = gathered_copies(cotangent[0], "tensor", 1)
    back_positions = row_positions(backward_routes[0], experts_here, groups, capacity)
    total_rows = experts_here * groups * capacity
    local_cot = cotangent[0]
    outgoing = place_rows(backward_gates[0], local_cot, back_positions, total_rows)
    received_part = lax.all_to_all(
        outgoing.reshape(experts_here, groups, capacity, local_cot.shape[1]),
        "expert",
        split_axis=1,
        concat_axis=1,
        tiled=True,
    )
    received = lax.all_gather(received_part, "tensor", axis=3, tiled=True)
    hidden_back = jnp.einsum(
        "egmd,ehd->egmh", received, weight, preferred_element_type=jnp.float32
    ).astype(jnp.bfloat16)
    shared_back = lax.dot_general(
        cotangent_whole,
        lax.all_gather(shared_piece, "expert", axis=1, tiled=True),
        (((1,), (1,)), ((), ())),
        preferred_element_type=jnp.float32,
    )
    return (handed[None], hidden_back[None], shared_back.astype(jnp.bfloat16)[None])


def solution(mesh):
    return jax.shard_map(
        on_device,
        mesh=mesh,
        in_specs=(
            P("phase", "expert", None),
            P("phase", "expert", None),
            P("phase", "expert", None, None, "tensor"),
            P("phase", "expert", "tensor", None),
            P("phase", "expert", "tensor"),
            P("phase", "tensor", "expert"),
            P("phase", "expert", None),
            P("phase", "expert", None),
            P("phase", "expert", "tensor"),
        ),
        out_specs=(
            P("phase", "expert", "tensor"),
            P("phase", "expert", None, None, "tensor"),
            P("phase", "expert", "tensor"),
        ),
        check_vma=False,
    )
```

profile of v0, /device:TPU:49, one launch (start us, length us, event | category | flops | bytes accessed | tf_op | source)
XLA Modules:
  0.0 391.0 jit_solution(6066048009045506084)
XLA Ops:
  7.2 0.7 copy.57
  7.9 0.8 copy.41
  8.7 0.1 convert_reduce_fusion
  8.8 0.1 reduce_window_sum.18
  8.9 0.3 select_reduce_fusion
  9.2 0.1 copy.42
  9.3 0.1 reduce_sum.65
  9.4 0.1 squeeze.23
  9.6 0.9 bitcast_convert_fusion
  10.6 0.1 mul.126
  10.7 0.1 copy.43
  10.8 0.1 mul.123
  11.0 2.4 scatter_custom_fusion
  13.4 0.2 reshape.228
  13.7 1.0 copy.44
  14.7 17.6 %all-to-all-start.2 = ((bf16[3,32,6,640]{3,2,0,1:T(8,128)(2,1)}), bf16[3,32,6,640]{3,2,0,1:T(8,128)(2,1)S(1)}, u32[]{:S(2)}, u32[]{:S(2)}) async-start(bf16[3,32,6,640]{3,2,0,1:T(8,128)(2,1)} %copy.44), calls=%async_computation.2 | async-start | bytes 1966080 | tf_op jit(solution)/shard_map/all_to_all | solution.py:105
  32.4 3.0 convolution_convert_fusion
  35.4 3.5 copy.35
  39.0 44.8 %all-to-all-done.2 = bf16[3,32,6,640]{3,2,0,1:T(8,128)(2,1)S(1)} async-done(((bf16[3,32,6,640]{3,2,0,1:T(8,128)(2,1)}), bf16[3,32,6,640]{3,2,0,1:T(8,128)(2,1)S(1)}, u32[]{:S(2)}, u32[]{:S(2)}) %all-to-all-start.2) | async-done | bytes 737312 | tf_op jit(solution)/shard_map/all_to_all | solution.py:105
  83.7 6.6 %all-to-all-start = ((bf16[3,32,6,2560]{3,2,0,1:T(8,128)(2,1)}), bf16[3,32,6,2560]{3,2,0,1:T(8,128)(2,1)}, u32[]{:S(2)}, u32[]{:S(2)}) async-start(bf16[3,32,6,2560]{3,2,0,1:T(8,128)(2,1)} %copy.35), calls=%async_computation | async-start | bytes 7864320 | tf_op jit(solution)/shard_map/all_to_all | solution.py:94
  90.4 0.7 all-gather.6.cloned.1.call-update
  91.2 1.0 copy.45
  92.2 198.5 %all-to-all-done = bf16[3,32,6,2560]{3,2,0,1:T(8,128)(2,1)} async-done(((bf16[3,32,6,2560]{3,2,0,1:T(8,128)(2,1)}), bf16[3,32,6,2560]{3,2,0,1:T(8,128)(2,1)}, u32[]{:S(2)}, u32[]{:S(2)}) %all-to-all-start) | async-done | bytes 2949152 | tf_op jit(solution)/shard_map/all_to_all | solution.py:94
  290.7 0.7 broadcast_in_dim.26
  291.5 4.3 %all-to-all-start.3 = ((bf16[4,64,640]{2,1,0:T(8,128)(2,1)}), bf16[4,64,640]{2,1,0:T(8,128)(2,1)}, u32[]{:S(2)}, u32[]{:S(2)}) async-start(bf16[4,64,640]{2,1,0:T(8,128)(2,1)} %broadcast_in_dim.26), calls=%async_computation.3 | async-start | bytes 655360 | tf_op jit(solution)/shard_map/all_to_all | solution.py:26
  295.7 0.1 convert_reduce_fusion.1
  295.9 0.1 copy.37
  296.0 0.1 reduce_window_sum.17
  296.1 0.3 select_reduce_fusion.1
  296.3 0.1 copy.38
  296.4 0.1 reduce_sum.60
  296.6 0.1 squeeze.22
  296.7 0.1 copy.48
  296.9 4.4 %copy.36 = bf16[3,32,6,2560]{3,2,1,0:T(8,128)(2,1)} copy(bf16[3,32,6,2560]{3,2,0,1:T(8,128)(2,1)} %all-to-all-done) | data formatting | bytes 5898240 | tf_op jit(solution)/shard_map/all_to_all | solution.py:94
  301.3 4.1 %reshape.226 = bf16[576,2560]{1,0:T(8,128)(2,1)S(1)} reshape(bf16[3,32,6,2560]{3,2,1,0:T(8,128)(2,1)} %copy.36) | data formatting | bytes 5898240 | tf_op jit(solution)/shard_map/reshape | solution.py:95
  305.4 3.3 gather_fusion
  308.6 4.5 %reshape.230 = f32[64,6,2560]{2,1,0:T(8,128)} reshape(bf16[384,2560]{1,0:T(8,128)(2,1)} %gather_fusion) | data formatting | bytes 5898240 | tf_op jit(solution)/shard_map/convert_element_type | solution.py:96
  313.1 4.8 %multiply_reduce_fusion = f32[64,2560]{1,0:T(8,128)S(1)} fusion(f32[64,6,2560]{2,1,0:T(8,128)} %reshape.230, f32[64,6]{1,0:T(8,128)S(1)} %bitcast.56), kind=kLoop, calls=%fused_computation.2 | loop fusion | flops 1802240 | bytes 4589056 | tf_op jit(solution)/shard_map/reduce_sum | solution.py:96
  317.9 2.4 convolution_add_fusion
  320.4 0.9 copy.56
  321.3 3.5 all-to-all-start.1
  324.7 1.0 copy.52
  325.8 1.1 fusion.15
  326.8 28.5 %all-to-all-done.1 = f32[4,64,640]{2,1,0:T(8,128)S(1)} async-done(((f32[4,64,640]{2,1,0:T(8,128)}), f32[4,64,640]{2,1,0:T(8,128)S(1)}, u32[]{:S(2)}, u32[]{:S(2)}) %all-to-all-start.1) | async-done | bytes 655392 | tf_op jit(solution)/shard_map/all_to_all | solution.py:14
  355.4 3.2 collective-permute-start
  358.6 19.8 %all-gather.4.cloned.1.call-done = bf16[3,32,6,2560]{3,1,2,0:T(8,128)(2,1)} async-done(((bf16[3,32,6,640]{3,1,2,0:T(8,128)(2,1)}), bf16[3,32,6,2560]{3,1,2,0:T(8,128)(2,1)}) %all-gather.4.cloned.1.call-update) | async-done | bytes 2949136 | tf_op jit(solution)/shard_map/all_gather | solution.py:112
  378.4 5.1 %fusion.9 = bf16[1,3,32,6,256]{4,2,3,1,0:T(8,128)(2,1)} fusion(bf16[3,32,6,2560]{3,1,2,0:T(8,128)(2,1)} %all-gather.4.cloned.1.call-done, bf16[1,3,256,2560]{3,2,1,0:T(8,128)(2,1)} %param.12), kind=kOutput, calls=%fused_computation.12 | convolution fusion | flops 755122176 | bytes 7176192 | tf_op jit(solution)/shard_map/egmd,ehd->egmh/dot_general | solution.py:113
  383.6 0.6 copy.60
  (28 shorter events, 0.4 us)
Async XLA Ops:
  7.2 25.2 %copy-start = (bf16[1,3,32,6,256]{4,2,3,1,0:T(8,128)(2,1)S(1)}, bf16[1,3,32,6,256]{4,2,3,1,0:T(8,128)(2,1)}, u32[]{:S(2)}) copy-start(bf16[1,3,32,6,256]{4,2,3,1,0:T(8,128)(2,1)} %param.11) | copy-start | bytes 884740
  7.2 3.6 copy-start.5
  14.7 69.0 %all-to-all-start.2 = ((bf16[3,32,6,640]{3,2,0,1:T(8,128)(2,1)}), bf16[3,32,6,640]{3,2,0,1:T(8,128)(2,1)S(1)}, u32[]{:S(2)}, u32[]{:S(2)}) async-start(bf16[3,32,6,640]{3,2,0,1:T(8,128)(2,1)} %copy.44), calls=%async_computation.2 | async-start | bytes 1966080 | tf_op jit(solution)/shard_map/all_to_all | solution.py:105
  39.0 53.3 %copy-start.4 = (s32[1,64,6]{1,0,2:T(1,128)S(1)}, s32[1,64,6]{1,0,2:T(1,128)}, u32[]{:S(2)}) copy-start(s32[1,64,6]{1,0,2:T(1,128)} %param.9) | copy-start | bytes 4612
  39.0 251.8 %copy-start.2 = (bf16[1,64,640]{2,1,0:T(8,128)(2,1)S(1)}, bf16[1,64,640]{2,1,0:T(8,128)(2,1)}, u32[]{:S(2)}) copy-start(bf16[1,64,640]{2,1,0:T(8,128)(2,1)} %param.17) | copy-start | bytes 245764
  83.7 207.0 %all-to-all-start = ((bf16[3,32,6,2560]{3,2,0,1:T(8,128)(2,1)}), bf16[3,32,6,2560]{3,2,0,1:T(8,128)(2,1)}, u32[]{:S(2)}, u32[]{:S(2)}) async-start(bf16[3,32,6,2560]{3,2,0,1:T(8,128)(2,1)} %copy.35), calls=%async_computation | async-start | bytes 7864320 | tf_op jit(solution)/shard_map/all_to_all | solution.py:94
  90.4 206.3 %copy-start.6 = (f32[1,64,6]{1,0,2:T(1,128)S(1)}, f32[1,64,6]{1,0,2:T(1,128)}, u32[]{:S(2)}) copy-start(f32[1,64,6]{1,0,2:T(1,128)} %param.10) | copy-start | bytes 4612
  90.4 227.5 %all-gather.6.cloned.1.call-start = ((), (), s32[]{:S(2)}) async-start(), calls=%async_computation.5 | async-start | bytes 2027520 | tf_op jit(solution)/shard_map/all_gather | solution.py:86
  91.1 287.3 %all-gather.4.cloned.1.call-start = ((), (), s32[]{:S(2)}) async-start(), calls=%async_computation.4 | async-start | bytes 3686400 | tf_op jit(solution)/shard_map/all_gather | solution.py:112
  291.5 29.8 %all-to-all-start.3 = ((bf16[4,64,640]{2,1,0:T(8,128)(2,1)}), bf16[4,64,640]{2,1,0:T(8,128)(2,1)}, u32[]{:S(2)}, u32[]{:S(2)}) async-start(bf16[4,64,640]{2,1,0:T(8,128)(2,1)} %broadcast_in_dim.26), calls=%async_computation.3 | async-start | bytes 655360 | tf_op jit(solution)/shard_map/all_to_all | solution.py:26
  313.1 4.8 %copy-start.3 = (bf16[1,64,384]{2,1,0:T(8,128)(2,1)S(1)}, bf16[1,64,384]{2,1,0:T(8,128)(2,1)}, u32[]{:S(2)}) copy-start(bf16[1,64,384]{2,1,0:T(8,128)(2,1)} %param.13) | copy-start | bytes 147460
  317.9 7.8 %copy-start.1 = (bf16[1,384,2560]{1,2,0:T(8,128)(2,1)S(1)}, bf16[1,384,2560]{1,2,0:T(8,128)(2,1)}, u32[]{:S(2)}) copy-start(bf16[1,384,2560]{1,2,0:T(8,128)(2,1)} %all-gather.6.cloned.1.call-done) | copy-start | bytes 5898244
  321.3 34.1 %all-to-all-start.1 = ((f32[4,64,640]{2,1,0:T(8,128)}), f32[4,64,640]{2,1,0:T(8,128)S(1)}, u32[]{:S(2)}, u32[]{:S(2)}) async-start(f32[4,64,640]{2,1,0:T(8,128)} %bitcast.50), calls=%async_computation.1 | async-start | bytes 1310720 | tf_op jit(solution)/shard_map/all_to_all | solution.py:14
  355.4 28.2 %collective-permute-start = (bf16[64,640]{1,0:T(8,128)(2,1)S(1)}, bf16[64,640]{1,0:T(8,128)(2,1)S(1)}, u32[]{:S(2)}, u32[]{:S(2)}) collective-permute-start(bf16[64,640]{1,0:T(8,128)(2,1)S(1)} %reduce_sum.62), channel_id=1, source_target_pairs={{0,128},{128,256},{256,384},{384,0},{1,129},{129,257},{257,385},{3... | collective-permute-start | bytes 245768 | tf_op jit(solution)/shard_map/ppermute | solution.py:21
Sparse Core Ops, SparseCore 0:
  94.4 201.1 all-gather.5
  297.8 80.5 all-gather.3
where the time goes:
time: 392 us; the launch traced here: 391 us
  waiting for transfers between devices  292 us (74%)
  starting transfers between devices  35.3 us (9%)
  local copies, waits for them, and re-layouts  28.3 us (7%)
  between operations  14.3 us (4%)
  matrix products  11.7 us (3%)
  other arithmetic  9.14 us (2%)
    all_to_all x1, waiting for transfers between devices, on_device(): lax.all_to_all(partial_value, 'expert', split_axis=1, concat_axis=1, tile...  198 us
    all_to_all x1, waiting for transfers between devices, on_device(): lax.all_to_all(outgoing.reshape(experts_here, groups, capacity, local_cot...  44.8 us
    all_to_all x1, waiting for transfers between devices, summed_on_arrival(): lax.all_to_all(parts, axis, split_axis=0, concat_axis=0, tiled=True)  28.5 us
    all_gather x1, waiting for transfers between devices, on_device(): received = lax.all_gather(received_part, 'tensor', axis=3, tiled=True)  19.8 us
    all_to_all x1, starting transfers between devices, on_device(): lax.all_to_all(outgoing.reshape(experts_here, groups, capacity, local_cot...  17.6 us
  transfers between devices with their start and end apart: 7, of which 4 were waited for; matrix products, arithmetic and copies ran while one was open for 10% of the time, Pallas kernels for 0%

commit v1 on v0

--- a/solution.py
+++ b/solution.py
@@ -109,7 +109,9 @@
         concat_axis=1,
         tiled=True,
     )
-    received = lax.all_gather(received_part, "tensor", axis=3, tiled=True)
+    received = jnp.concatenate(
+        lax.all_to_all(jnp.stack([received_part] * lax.axis_size("tensor")), "tensor", 0, 0), axis=3
+    )
     hidden_back = jnp.einsum(
         "egmd,ehd->egmh", received, weight, preferred_element_type=jnp.float32
     ).astype(jnp.bfloat16)

time: 392 us -> 446 us (1.14)
  the two profiles are of different devices: /device:TPU:49 before, /device:TPU:1 now
where the time goes in v1:
time: 446 us; the launch traced here: 444 us
  waiting for transfers between devices  328 us (74%)
  starting transfers between devices  49.4 us (11%)
  local copies, waits for them, and re-layouts  32.5 us (7%)
  between operations  14.3 us (3%)
  matrix products  10.8 us (2%)
  other arithmetic  9.87 us (2%)
    all_to_all x1, waiting for transfers between devices, on_device(): lax.all_to_all(partial_value, 'expert', split_axis=1, concat_axis=1, tile...  174 us
    all_gather x1, waiting for transfers between devices, on_device(): lax.all_gather(shared_piece, 'expert', axis=1, tiled=True)  97.4 us
    all_to_all x1, waiting for transfers between devices, on_device(): lax.all_to_all(outgoing.reshape(experts_here, groups, capacity, local_cot...  42.8 us
    all_to_all x1, starting transfers between devices, on_device(): lax.all_to_all(outgoing.reshape(experts_here, groups, capacity, local_cot...  20.2 us
    all_to_all x1, waiting for transfers between devices, summed_on_arrival(): lax.all_to_all(parts, axis, split_axis=0, concat_axis=0, tiled=True)  12.9 us
  transfers between devices with their start and end apart: 7, of which 4 were waited for; matrix products, arithmetic and copies ran while one was open for 11% of the time, Pallas kernels for 0%

profile of v1, /device:TPU:1, one launch (start us, length us, event | category | flops | bytes accessed | tf_op | source)
XLA Modules:
  0.0 444.5 jit_solution(11174500284585571571)
XLA Ops:
  7.2 1.7 broadcast_in_dim.26
  8.9 6.4 %all-to-all-start.4 = ((bf16[4,64,640]{2,1,0:T(8,128)(2,1)}), bf16[4,64,640]{2,1,0:T(8,128)(2,1)}, u32[]{:S(2)}, u32[]{:S(2)}) async-start(bf16[4,64,640]{2,1,0:T(8,128)(2,1)} %broadcast_in_dim.26), calls=%async_computation.4 | async-start | bytes 655360 | tf_op jit(solution)/shard_map/all_to_all | solution.py:26
  15.3 0.7 copy.60
  16.0 0.8 copy.42
  16.8 0.1 convert_reduce_fusion
  17.0 0.3 select_reduce_fusion
  17.3 0.1 copy.43
  17.4 0.1 reduce_sum.65
  17.5 0.1 squeeze.23
  17.7 0.9 bitcast_convert_fusion
  18.7 0.1 mul.126
  18.8 0.1 copy.44
  18.9 0.1 mul.123
  19.1 2.4 scatter_custom_fusion
  21.5 0.2 reshape.236
  21.8 1.0 copy.45
  22.8 20.2 %all-to-all-start.2 = ((bf16[3,32,6,640]{3,2,0,1:T(8,128)(2,1)}), bf16[3,32,6,640]{3,2,0,1:T(8,128)(2,1)S(1)}, u32[]{:S(2)}, u32[]{:S(2)}) async-start(bf16[3,32,6,640]{3,2,0,1:T(8,128)(2,1)} %copy.45), calls=%async_computation.2 | async-start | bytes 1966080 | tf_op jit(solution)/shard_map/all_to_all | solution.py:105
  43.1 3.1 convolution_convert_fusion
  46.1 3.5 copy.36
  49.7 42.8 %all-to-all-done.2 = bf16[3,32,6,640]{3,2,0,1:T(8,128)(2,1)S(1)} async-done(((bf16[3,32,6,640]{3,2,0,1:T(8,128)(2,1)}), bf16[3,32,6,640]{3,2,0,1:T(8,128)(2,1)S(1)}, u32[]{:S(2)}, u32[]{:S(2)}) %all-to-all-start.2) | async-done | bytes 737312 | tf_op jit(solution)/shard_map/all_to_all | solution.py:105
  92.4 8.8 %all-to-all-start = ((bf16[3,32,6,2560]{3,2,0,1:T(8,128)(2,1)}), bf16[3,32,6,2560]{3,2,0,1:T(8,128)(2,1)}, u32[]{:S(2)}, u32[]{:S(2)}) async-start(bf16[3,32,6,2560]{3,2,0,1:T(8,128)(2,1)} %copy.36), calls=%async_computation | async-start | bytes 7864320 | tf_op jit(solution)/shard_map/all_to_all | solution.py:94
  101.4 173.9 %all-to-all-done = bf16[3,32,6,2560]{3,2,0,1:T(8,128)(2,1)} async-done(((bf16[3,32,6,2560]{3,2,0,1:T(8,128)(2,1)}), bf16[3,32,6,2560]{3,2,0,1:T(8,128)(2,1)}, u32[]{:S(2)}, u32[]{:S(2)}) %all-to-all-start) | async-done | bytes 2949152 | tf_op jit(solution)/shard_map/all_to_all | solution.py:94
  275.2 2.0 stack.2
  277.3 6.1 %all-to-all-start.3 = ((bf16[4,3,32,6,640]{4,2,3,1,0:T(8,128)(2,1)}), bf16[4,3,32,6,640]{4,2,3,1,0:T(8,128)(2,1)}, u32[]{:S(2)}, u32[]{:S(2)}) async-start(bf16[4,3,32,6,640]{4,2,3,1,0:T(8,128)(2,1)} %stack.2), calls=%async_computation.3 | async-start | bytes 5898240 | tf_op jit(solution)/shard_map/all_to_all | solution.py:113
  283.3 0.7 all-gather.3.cloned.1.call-update
  284.1 0.1 copy.38
  284.2 0.1 convert_reduce_fusion.1
  284.4 0.3 select_reduce_fusion.1
  284.7 0.1 copy.39
  284.8 0.1 reduce_sum.60
  284.9 0.1 squeeze.22
  285.2 4.4 copy.37
  289.6 4.1 reshape.234
  293.7 3.3 gather_fusion
  297.0 4.5 %reshape.240 = f32[64,6,2560]{2,1,0:T(8,128)} reshape(bf16[384,2560]{1,0:T(8,128)(2,1)} %gather_fusion) | data formatting | bytes 5898240 | tf_op jit(solution)/shard_map/convert_element_type | solution.py:96
  301.5 4.4 multiply_reduce_fusion
  305.9 97.4 %all-gather.3.cloned.1.call-done = bf16[1,384,2560]{1,2,0:T(8,128)(2,1)} async-done(((bf16[1,384,80]{1,2,0:T(8,128)(2,1)}), bf16[1,384,2560]{1,2,0:T(8,128)(2,1)}) %all-gather.3.cloned.1.call-update) | async-done | bytes 1966096 | tf_op jit(solution)/shard_map/all_gather | solution.py:86
  403.3 2.4 convolution_add_fusion
  405.7 0.9 copy.59
  406.6 4.2 all-to-all-start.1
  410.8 1.0 copy.55
  411.8 1.1 fusion.15
  412.9 2.2 copy.54
  415.1 12.9 %all-to-all-done.1 = f32[4,64,640]{2,1,0:T(8,128)} async-done(((f32[4,64,640]{2,1,0:T(8,128)}), f32[4,64,640]{2,1,0:T(8,128)}, u32[]{:S(2)}, u32[]{:S(2)}) %all-to-all-start.1) | async-done | bytes 655392 | tf_op jit(solution)/shard_map/all_to_all | solution.py:14
  428.0 1.1 reduce_sum.62
  429.1 3.6 collective-permute-start
  432.8 4.2 fusion.9
  437.0 0.6 copy.63
  (27 shorter events, 0.6 us)
Async XLA Ops:
  7.2 35.9 %copy-start = (bf16[1,3,32,6,256]{4,2,3,1,0:T(8,128)(2,1)S(1)}, bf16[1,3,32,6,256]{4,2,3,1,0:T(8,128)(2,1)}, u32[]{:S(2)}) copy-start(bf16[1,3,32,6,256]{4,2,3,1,0:T(8,128)(2,1)} %param.11) | copy-start | bytes 884740
  7.2 11.6 %copy-start.4 = (f32[1,64,6]{1,0,2:T(1,128)S(1)}, f32[1,64,6]{1,0,2:T(1,128)}, u32[]{:S(2)}) copy-start(f32[1,64,6]{1,0,2:T(1,128)} %param.16) | copy-start | bytes 4612
  8.9 13.9 %all-to-all-start.4 = ((bf16[4,64,640]{2,1,0:T(8,128)(2,1)}), bf16[4,64,640]{2,1,0:T(8,128)(2,1)}, u32[]{:S(2)}, u32[]{:S(2)}) async-start(bf16[4,64,640]{2,1,0:T(8,128)(2,1)} %broadcast_in_dim.26), calls=%async_computation.4 | async-start | bytes 655360 | tf_op jit(solution)/shard_map/all_to_all | solution.py:26
  22.8 69.6 %all-to-all-start.2 = ((bf16[3,32,6,640]{3,2,0,1:T(8,128)(2,1)}), bf16[3,32,6,640]{3,2,0,1:T(8,128)(2,1)S(1)}, u32[]{:S(2)}, u32[]{:S(2)}) async-start(bf16[3,32,6,640]{3,2,0,1:T(8,128)(2,1)} %copy.45), calls=%async_computation.2 | async-start | bytes 1966080 | tf_op jit(solution)/shard_map/all_to_all | solution.py:105
  92.4 182.8 %all-to-all-start = ((bf16[3,32,6,2560]{3,2,0,1:T(8,128)(2,1)}), bf16[3,32,6,2560]{3,2,0,1:T(8,128)(2,1)}, u32[]{:S(2)}, u32[]{:S(2)}) async-start(bf16[3,32,6,2560]{3,2,0,1:T(8,128)(2,1)} %copy.36), calls=%async_computation | async-start | bytes 7864320 | tf_op jit(solution)/shard_map/all_to_all | solution.py:94
  277.2 6.8 %copy-start.3 = (s32[1,64,6]{1,0,2:T(1,128)S(1)}, s32[1,64,6]{1,0,2:T(1,128)}, u32[]{:S(2)}) copy-start(s32[1,64,6]{1,0,2:T(1,128)} %param.9) | copy-start | bytes 4612
  277.2 7.8 %copy-start.5 = (f32[1,64,6]{1,0,2:T(1,128)S(1)}, f32[1,64,6]{1,0,2:T(1,128)}, u32[]{:S(2)}) copy-start(f32[1,64,6]{1,0,2:T(1,128)} %param.10) | copy-start | bytes 4612
  277.3 129.3 %all-to-all-start.3 = ((bf16[4,3,32,6,640]{4,2,3,1,0:T(8,128)(2,1)}), bf16[4,3,32,6,640]{4,2,3,1,0:T(8,128)(2,1)}, u32[]{:S(2)}, u32[]{:S(2)}) async-start(bf16[4,3,32,6,640]{4,2,3,1,0:T(8,128)(2,1)} %stack.2), calls=%async_computation.3 | async-start | bytes 5898240 | tf_op jit(solution)/shard_map/all_to_all | solution.py:113
  283.3 119.9 %all-gather.3.cloned.1.call-start = ((), (), s32[]{:S(2)}) async-start(), calls=%async_computation.5 | async-start | bytes 2027520 | tf_op jit(solution)/shard_map/all_gather | solution.py:86
  301.5 101.8 %copy-start.2 = (bf16[1,64,384]{2,1,0:T(8,128)(2,1)S(1)}, bf16[1,64,384]{2,1,0:T(8,128)(2,1)}, u32[]{:S(2)}) copy-start(bf16[1,64,384]{2,1,0:T(8,128)(2,1)} %param.13) | copy-start | bytes 147460
  403.3 8.5 %copy-start.1 = (bf16[1,384,2560]{1,2,0:T(8,128)(2,1)S(1)}, bf16[1,384,2560]{1,2,0:T(8,128)(2,1)}, u32[]{:S(2)}) copy-start(bf16[1,384,2560]{1,2,0:T(8,128)(2,1)} %all-gather.3.cloned.1.call-done) | copy-start | bytes 5898244
  406.6 21.4 %all-to-all-start.1 = ((f32[4,64,640]{2,1,0:T(8,128)}), f32[4,64,640]{2,1,0:T(8,128)}, u32[]{:S(2)}, u32[]{:S(2)}) async-start(f32[4,64,640]{2,1,0:T(8,128)} %bitcast.53), calls=%async_computation.1 | async-start | bytes 1310720 | tf_op jit(solution)/shard_map/all_to_all | solution.py:14
  429.1 7.9 %collective-permute-start = (bf16[64,640]{1,0:T(8,128)(2,1)S(1)}, bf16[64,640]{1,0:T(8,128)(2,1)S(1)}, u32[]{:S(2)}, u32[]{:S(2)}) collective-permute-start(bf16[64,640]{1,0:T(8,128)(2,1)S(1)} %reduce_sum.62), channel_id=1, source_target_pairs={{0,128},{128,256},{256,384},{384,0},{1,129},{129,257},{257,385},{3... | collective-permute-start | bytes 245768 | tf_op jit(solution)/shard_map/ppermute | solution.py:21
Sparse Core Ops, SparseCore 0:
  287.4 115.8 all-gather.2
